TPU v7x, 128 devices: a whole 4x4x4 slice. The times are simulated.
128 devices in a mesh: clip: 4 (over y_hi, core), tile: 32 (over y_lo, x, z).
Axes of the slice: x: 4, y: 4 (y_hi: 2, y_lo: 2; y = y_hi * 2 + y_lo), z: 4, core: 2. Of those that a mesh axis runs over, the one named last changes fastest.
Arguments:
- features: bfloat16 [8, 16, 64, 12, 384], P('clip', None, 'tile'), may hold values from -6 to 6
- pixel_grad: bfloat16 [8, 16, 64, 12, 384], P('clip', None, 'tile'), may hold values from -6 to 6
- frame_list: int32 [8, 16], P('clip'), may hold values from -1 to 15, as said below
- conv_weight: bfloat16 [3, 3, 3, 384, 384], replicated, may hold values from -0.0625 to 0.0625
- in_weight: bfloat16 [3, 3, 3, 16, 384], replicated, may hold values from -0.3125 to 0.3125
- last_hidden: bfloat16 [24576, 5120], P(('clip', 'tile')), may hold values from -6 to 6
- modulation: float32 [8, 2, 5120], P('clip'), may hold values from -3 to 3
- head_weight: bfloat16 [5120, 64], replicated, may hold values from -0.75 to 0.75
Outputs:
- hidden_grad: bfloat16 [24576, 5120], P(('clip', 'tile'))
- head_weight_grad: float32 [5120, 64], replicated
- modulation_grad: float32 [8, 2, 5120], P('clip')
- conv_weight_grad: float32 [3, 3, 3, 384, 384], P(None, None, None, 'tile')
Inputs may be any that keep to these rules, and one draw needn't show every extreme that they name: `frame_list`: each clip's list holds between 2 and 16 distinct frame numbers first, then -1; some clip lists every frame.
All inputs are finite; a program needn't handle non-finite values.
Results may differ from a plain program's by a relative error of at most 0.006.
Values may be sent and summed in bfloat16 or wider, within the bound.
No kernel may reach another device: no remote copies, remote signals or barrier semaphores. Data moves between devices by JAX's collectives and lax.ppermute only.
A program may use at most 192 MiB of HBM per device.

v0:
```python
import jax
import jax.numpy as jnp
from jax import lax
from jax.sharding import PartitionSpec as P


def padded(block, sides, width):
    for axis, dim in sides:
        count = lax.axis_size(axis)
        forward = [(i, i + 1) for i in range(count - 1)]
        backward = [(target, source) for source, target in forward]
        low = lax.ppermute(
            lax.slice_in_dim(block, block.shape[dim] - width, None, axis=dim), axis, forward
        )
        high = lax.ppermute(lax.slice_in_dim(block, 0, width, axis=dim), axis, backward)
        block = jnp.concatenate([low, block, high], axis=dim)
    return block


def silu_slope(values):
    sig = jax.nn.sigmoid(values)
    return sig * (1.0 + values * (1.0 - sig))


def shifted(padded_grad, out_rows, row_taps):
    frames = padded_grad.shape[1]
    columns = padded_grad.shape[3]
    widened = jnp.pad(padded_grad, ((0, 0), (0, 2), (0, 0), (1, 1), (0, 0)))
    windows = []
    for time_tap in range(3):
        for row_tap in row_taps:
            for col_tap in (-1, 0, 1):
                window = widened[
                    :,
                    time_tap : time_tap + frames,
                    1 - row_tap : 1 - row_tap + out_rows,
                    1 - col_tap : 1 - col_tap + columns,
                    :,
                ]
                windows.append(((time_tap, row_tap + 1, col_tap + 1), window))
    return windows


def conv_back(padded_grad, weight, out_rows, row_taps):
    summed = None
    shape = None
    for (time_tap, row_tap, col_tap), window in shifted(padded_grad, out_rows, row_taps):
        shape = window.shape[:-1] + (weight.shape[3],)
        product = jnp.dot(
            window.reshape(-1, window.shape[-1]),
            weight[time_tap, row_tap, col_tap].T,
            preferred_element_type=jnp.float32,
        )
        summed = product if summed is None else summed + product
    return summed.reshape(shape)


def weight_grad(activations, padded_grad, out_rows):
    flattened = activations.reshape(-1, activations.shape[-1])
    gradients = [
        jnp.dot(
            flattened.T, window.reshape(-1, window.shape[-1]), preferred_element_type=jnp.float32
        )
        for _, window in shifted(padded_grad, out_rows, (-1, 0, 1))
    ]
    return jnp.stack(gradients).reshape(3, 3, 3, flattened.shape[1], padded_grad.shape[-1])


def local(
    features, pixel_grad, frame_list, conv_weight, in_weight, last_hidden, modulation, head_weight
):
    clip_here, frames, rows_here, columns, _ = features.shape
    width = last_hidden.shape[1]
    scored = jnp.any(
        frame_list[:, None, :] == jnp.arange(frames, dtype=jnp.int32)[None, :, None], axis=-1
    )
    masked = pixel_grad * scored.astype(jnp.bfloat16)[:, :, None, None, None]
    feats = features.astype(jnp.float32)
    activation = jax.nn.silu(feats).astype(jnp.bfloat16)
    slopes = silu_slope(feats)
    grad_rim = padded(masked, (("tile", 2),), 1)
    grad_act = conv_back(grad_rim, conv_weight, rows_here, (-1, 0, 1))
    partial_w = weight_grad(activation, grad_rim, rows_here)
    share_w = lax.psum_scatter(partial_w, "tile", scatter_dimension=3, tiled=True)
    conv_weight_grad = lax.psum(share_w, "clip")
    grad_feat = (grad_act * slopes).astype(jnp.bfloat16)
    feat_rim = padded(grad_feat, (("tile", 2),), 1)
    latent = conv_back(feat_rim, in_weight, rows_here, (-1, 0, 1))
    latent_grad = latent.astype(jnp.bfloat16)
    channels = latent_grad.shape[-1]
    patches = latent_grad.reshape(clip_here * frames, rows_here // 2, 2, columns // 2, 2, channels)
    patches = jnp.transpose(patches, (0, 1, 3, 2, 4, 5)).reshape(
        clip_here * frames, rows_here // 2, columns // 2, 4 * channels
    )
    tokens_grad = lax.all_to_all(patches, "tile", split_axis=0, concat_axis=1, tiled=True)
    blocks_here = tokens_grad.shape[0]
    per_block = tokens_grad.shape[1] * tokens_grad.shape[2]
    patch_grad = tokens_grad.reshape(-1, 4 * channels)
    block_ids = lax.axis_index("tile") * blocks_here + jnp.arange(blocks_here, dtype=jnp.int32)
    onehot = (
        block_ids[:, None] // frames == jnp.arange(clip_here, dtype=jnp.int32)[None, :]
    ).astype(jnp.float32)
    mods = jnp.einsum("kc,cad->kad", onehot, modulation, precision=lax.Precision.HIGHEST)
    states = last_hidden.reshape(blocks_here, per_block, width).astype(jnp.float32)
    average = jnp.mean(states, axis=-1, keepdims=True)
    centered = states - average
    inv_std = lax.rsqrt(jnp.mean(centered * centered, axis=-1, keepdims=True) + 1e-06)
    normed = centered * inv_std
    head_input = (normed * (1.0 + mods[:, 1][:, None, :]) + mods[:, 0][:, None, :]).astype(
        jnp.bfloat16
    )
    partial_head = jnp.dot(
        head_input.reshape(-1, width).T, patch_grad, preferred_element_type=jnp.float32
    )
    grad_input = jnp.dot(patch_grad, head_weight.T, preferred_element_type=jnp.float32).reshape(
        blocks_here, per_block, width
    )
    block_terms = jnp.stack(
        [jnp.sum(grad_input, axis=1), jnp.sum(grad_input * normed, axis=1)], axis=1
    )
    clip_terms = jnp.einsum("kc,kad->cad", onehot, block_terms, precision=lax.Precision.HIGHEST)
    head_weight_grad = lax.psum(partial_head, ("clip", "tile"))
    modulation_grad = lax.psum(clip_terms, "tile")
    scaled = grad_input * (1.0 + mods[:, 1][:, None, :])
    result = (
        scaled
        - jnp.mean(scaled, axis=-1, keepdims=True)
        - normed * jnp.mean(scaled * normed, axis=-1, keepdims=True)
    ) * inv_std
    hidden_grad = result.astype(jnp.bfloat16).reshape(-1, width)
    return (hidden_grad, head_weight_grad, modulation_grad, conv_weight_grad)


def solution(mesh):
    return jax.shard_map(
        local,
        mesh=mesh,
        in_specs=(
            P("clip", None, "tile", None, None),
            P("clip", None, "tile", None, None),
            P("clip", None),
            P(),
            P(),
            P(("clip", "tile"), None),
            P("clip", None, None),
            P(),
        ),
        out_specs=(
            P(("clip", "tile"), None),
            P(),
            P("clip", None, None),
            P(None, None, None, "tile", None),
        ),
        check_vma=False,
    )
```

profile of v0, /device:TPU:1, one launch (start us, length us, event | category | flops | bytes accessed | tf_op | source)
XLA Modules:
  0.0 960.4 jit_solution(16089638649038633507)
XLA Ops:
  10.7 5.8 collective-permute-start
  18.4 2.2 fusion.13
  22.7 2.5 fusion.159
  26.1 2.1 fusion.33
  28.2 2.3 fusion.337
  30.5 6.2 fusion.336
  36.8 2.0 reshape.359
  38.8 2.7 fusion.116
  43.4 2.7 fusion.118
  48.1 2.7 fusion.120
  52.8 2.7 fusion.122
  57.4 2.7 fusion.124
  62.1 2.7 fusion.126
  66.8 2.7 fusion.128
  71.5 2.8 fusion.130
  76.2 2.8 fusion.132
  81.0 2.7 fusion.134
  85.7 2.7 fusion.136
  90.4 2.7 fusion.138
  95.1 2.7 fusion.140
  97.8 2.0 reshape.346
  99.8 2.7 fusion.142
  102.5 2.2 reshape.345
  104.7 2.7 fusion.144
  109.4 2.7 fusion.146
  114.0 2.7 fusion.148
  118.7 2.7 fusion.150
  123.4 2.7 fusion.152
  126.1 2.4 pad_maximum_fusion.3
  129.8 2.6 fusion.154
  132.4 2.1 reshape.339
  134.5 2.7 fusion.156
  138.1 2.1 reshape.336
  140.2 2.7 fusion.161
  143.9 2.8 fusion.163
  146.7 2.1 reshape.333
  148.7 2.7 fusion.167
  154.2 12.1 %fusion.66 = f32[768,384]{1,0:T(8,128)} fusion(f32[768,384]{1,0:T(8,128)} %fusion.116, f32[768,384]{1,0:T(8,128)} %fusion.118, f32[768,384]{1,0:T(8,128)} %fusion.120, f32[768,384]{1,0:T(8,128)} %fusion.122, f32[768,384]{1,0:T(8,128)} %fusion.124, f32[768,384]{1,0:T(8,128)} %fusion.126, f32[768,384]{1,0:T(8,128)} %fusion.128, f32[768,384]{1,0:T(8,128)} %fusion.130, ...), kind=kOutput, calls=%fused_computation.75 | convolution fusion | flops 234160128 | bytes 32735232 | tf_op jit(solution)/shard_map/dot_general | solution.py:49
  166.3 2.5 reshape.360
  173.4 5.2 collective-permute-start.2
  223.4 2.3 fusion.335
  225.7 6.2 fusion.334
  231.9 2.0 reshape.387
  235.2 2.0 reshape.386
  238.6 2.0 reshape.385
  241.9 2.0 reshape.384
  245.2 2.0 reshape.383
  248.6 2.0 reshape.382
  251.9 2.0 reshape.381
  303.3 2.6 pad_maximum_fusion.1
  305.9 2.1 reshape.368
  312.8 2.1 reshape.366
  319.8 2.0 fusion.247
  328.2 2.3 fusion.115
  332.3 14.4 %all-to-all-start = ((bf16[32,2,192]{2,1,0:T(2,128)(2,1)}), bf16[32,2,192]{2,1,0:T(2,128)(2,1)S(1)}, u32[]{:S(2)}, u32[]{:S(2)}) async-start(bf16[32,2,192]{2,1,0:T(2,128)(2,1)} %reshape.426), calls=%async_computation | async-start | bytes 65536 | tf_op jit(solution)/shard_map/all_to_all | solution.py:95
  348.5 5.4 all-to-all-done
  354.1 5.0 fusion.12
  360.6 3.6 fusion.22
  365.6 376.7 %all-reduce.12.cloned.1.call-done = (f32[2,2,5120]{2,1,0:T(2,128)}, f32[3,3,3,384,384]{4,3,2,1,0:T(8,128)}) async-done(((f32[2,2,5120]{2,1,0:T(2,128)}, f32[3,3,3,384,384]{4,3,2,1,0:T(8,128)}), (f32[2,2,5120]{2,1,0:T(2,128)}, f32[3,3,3,384,384]{4,3,2,1,0:T(8,128)})) %all-reduce.12.cloned.1.call-update) | async-done | bytes 16007184 | tf_op jit(solution)/shard_map/psum | solution.py:123
  742.3 2.1 constant_dynamic-slice_fusion
  744.4 5.6 fusion.9
  750.0 154.9 %all-reduce.8.cloned.1.call-done = f32[5120,64]{0,1:T(8,128)} async-done(((f32[5120,64]{0,1:T(8,128)}), f32[5120,64]{0,1:T(8,128)}) %all-reduce.8.cloned.1.call-update) | async-done | bytes 1310736 | tf_op jit(solution)/shard_map/psum | solution.py:122
  904.9 44.7 %all-reduce.10.cloned.1.call-done = f32[3,3,3,12,384]{4,3,2,1,0:T(8,128)} async-done(((f32[3,3,3,12,384]{4,3,2,1,0:T(8,128)}), f32[3,3,3,12,384]{4,3,2,1,0:T(8,128)}) %all-reduce.10.cloned.1.call-update) | async-done | bytes 497680 | tf_op jit(solution)/shard_map/psum | solution.py:85
  949.6 2.5 copy.206
  (187 shorter events, 176.1 us)
Async XLA Ops:
  7.2 346.9 %copy-start = (bf16[5120,64]{0,1:T(8,128)(2,1)S(1)}, bf16[5120,64]{0,1:T(8,128)(2,1)}, u32[]{:S(2)}) copy-start(bf16[5120,64]{0,1:T(8,128)(2,1)} %param.15) | copy-start | bytes 1966084
  9.4 15.9 %collective-permute-start.1 = (bf16[2,16,1,12,384]{4,3,2,1,0:T(8,128)(2,1)S(1)}, bf16[2,16,1,12,384]{4,3,2,1,0:T(8,128)(2,1)S(1)}, u32[]{:S(2)}, u32[]{:S(2)}) collective-permute-start(bf16[2,16,1,12,384]{4,3,2,1,0:T(8,128)(2,1)S(1)} %get-tuple-element.65), channel_id=1, source_target_pairs={{1,0},{2,1},{3,2},{4,3},{5,4},{6,5},{7,6},{8,7},{9,8},{10,9},{11,1... | collective-permute-start | bytes 884744 | tf_op jit(solution)/shard_map/ppermute | solution.py:15
  10.7 15.4 %collective-permute-start = (bf16[2,16,1,12,384]{4,3,2,1,0:T(8,128)(2,1)S(1)}, bf16[2,16,1,12,384]{4,3,2,1,0:T(8,128)(2,1)}, u32[]{:S(2)}, u32[]{:S(2)}) collective-permute-start(bf16[2,16,1,12,384]{4,3,2,1,0:T(8,128)(2,1)S(1)} %get-tuple-element.64), channel_id=1, source_target_pairs={{0,1},{1,2},{2,3},{3,4},{4,5},{5,6},{6,7},{7,8},{8,9},{9,10},{10,1... | collective-permute-start | bytes 884744 | tf_op jit(solution)/shard_map/ppermute | solution.py:12
  16.4 4.7 copy-start.26
  18.4 2.8 copy-start.22
  21.4 0.6 copy-start.21
  25.3 0.8 copy-start.12
  123.4 2.8 copy-start.13
  132.4 4.8 copy-start.9
  138.1 4.8 copy-start.8
  146.7 4.8 copy-start.4
  152.4 1.8 copy-start.2
  152.4 1.8 copy-start.11
  166.3 2.5 copy-start.16
  168.8 1.7 copy-start.1
  168.8 1.7 copy-start.17
  170.5 8.1 copy-start.5
  172.1 49.3 %collective-permute-start.3 = (bf16[2,16,1,12,384]{4,3,2,1,0:T(8,128)(2,1)}, bf16[2,16,1,12,384]{4,3,2,1,0:T(8,128)(2,1)}, u32[]{:S(2)}, u32[]{:S(2)}) collective-permute-start(bf16[2,16,1,12,384]{4,3,2,1,0:T(8,128)(2,1)} %get-tuple-element.61), channel_id=1, source_target_pairs={{1,0},{2,1},{3,2},{4,3},{5,4},{6,5},{7,6},{8,7},{9,8},{10,9},{11,1... | collective-permute-start | bytes 884744 | tf_op jit(solution)/shard_map/ppermute | solution.py:15
  173.4 48.0 %collective-permute-start.2 = (bf16[2,16,1,12,384]{4,3,2,1,0:T(8,128)(2,1)}, bf16[2,16,1,12,384]{4,3,2,1,0:T(8,128)(2,1)}, u32[]{:S(2)}, u32[]{:S(2)}) collective-permute-start(bf16[2,16,1,12,384]{4,3,2,1,0:T(8,128)(2,1)} %get-tuple-element.60), channel_id=1, source_target_pairs={{0,1},{1,2},{2,3},{3,4},{4,5},{5,6},{6,7},{7,8},{8,9},{9,10},{10,1... | collective-permute-start | bytes 884744 | tf_op jit(solution)/shard_map/ppermute | solution.py:12
  181.5 1.7 copy-start.15
  186.4 1.7 copy-start.3
  305.9 4.0 copy-start.10
  312.8 6.0 copy-start.7
  319.8 6.0 copy-start.6
  326.8 20.3 %copy-start.18 = (bf16[2,16,2,12,384]{4,2,3,1,0:T(2,128)(2,1)S(1)}, bf16[2,16,2,12,384]{4,2,3,1,0:T(2,128)(2,1)}, u32[]{:S(2)}) copy-start(bf16[2,16,2,12,384]{4,2,3,1,0:T(2,128)(2,1)} %param.8) | copy-start | bytes 1769476
  332.3 21.6 %all-to-all-start = ((bf16[32,2,192]{2,1,0:T(2,128)(2,1)}), bf16[32,2,192]{2,1,0:T(2,128)(2,1)S(1)}, u32[]{:S(2)}, u32[]{:S(2)}) async-start(bf16[32,2,192]{2,1,0:T(2,128)(2,1)} %reshape.426), calls=%async_computation | async-start | bytes 65536 | tf_op jit(solution)/shard_map/all_to_all | solution.py:95
  346.7 7.3 copy-start.19
  346.8 7.3 copy-start.23
  346.8 7.3 copy-start.24
  346.8 395.5 %all-reduce.12.cloned.1.call-start = ((), (), s32[]{:S(2)}) async-start(), calls=%async_computation.3 | async-start | bytes 32014336 | tf_op jit(solution)/shard_map/psum | solution.py:123
  354.1 5.1 copy-start.25
  359.9 0.7 slice-start
  359.9 545.0 %all-reduce.8.cloned.1.call-start = ((), (), s32[]{:S(2)}) async-start(), calls=%async_computation.1 | async-start | bytes 2621440 | tf_op jit(solution)/shard_map/psum | solution.py:122
  360.6 3.7 copy-start.27
  364.3 585.4 %all-reduce.10.cloned.1.call-start = ((), (), s32[]{:S(2)}) async-start(), calls=%async_computation.2 | async-start | bytes 1327104 | tf_op jit(solution)/shard_map/psum | solution.py:85
  750.0 202.1 %copy-start.20 = (f32[2,2,5120]{2,1,0:T(2,128)S(1)}, f32[2,2,5120]{2,1,0:T(2,128)}, u32[]{:S(2)}) copy-start(f32[2,2,5120]{2,1,0:T(2,128)} %get-tuple-element.71) | copy-start | bytes 245764
  949.6 3.2 copy-start.14
Sparse Core Ops, SparseCore 0:
  360.0 382.2 all-reduce.11
  748.4 156.4 all-reduce.7
  908.0 41.5 all-reduce.9
where the time goes:
time: 966 us; the launch traced here: 960 us
  waiting for transfers between devices  582 us (60%)
  matrix products  182 us (19%)
  local copies, waits for them, and re-layouts  129 us (13%)
  starting transfers between devices  28.3 us (3%)
  other arithmetic  24 us (2%)
  between operations  15 us (2%)
    psum x1, waiting for transfers between devices, local(): modulation_grad = lax.psum(clip_terms, 'tile')  377 us
    psum x1, waiting for transfers between devices, local(): head_weight_grad = lax.psum(partial_head, ('clip', 'tile'))  155 us
    dot_general x54, matrix products, conv_back(): jnp.dot(window.reshape(-1, window.shape[-1]), weight[time_tap, row_tap, c...  130 us
    reshape x54, local copies, waits for them, and re-layouts, conv_back(): window.reshape(-1, window.shape[-1])  98.2 us
    psum x1, waiting for transfers between devices, local(): conv_weight_grad = lax.psum(share_w, 'clip')  44.7 us
    dot_general x27, matrix products, weight_grad(): jnp.dot(flattened.T, window.reshape(-1, window.shape[-1]), preferred_elem...  43.6 us
  transfers between devices with their start and end apart: 8, of which 4 were waited for; matrix products, arithmetic and copies ran while one was open for 7% of the time, Pallas kernels for 0%

commit v1 on v0

v1 whole, which is shorter than its diff:
```python
import functools

import jax
import jax.numpy as jnp
from jax import lax
from jax.experimental import pallas as pl
from jax.experimental.pallas import tpu as pltpu
from jax.sharding import PartitionSpec as P

F32 = jnp.float32
BF16 = jnp.bfloat16
BOTH = ("clip", "tile")
FRAMES = 16
SPAN = 32
COLS = 12
CH = 384
WIDTH = 5120
HALF = 2560
STEP = 512
PIECE = 384
LOAD = HALF + PIECE
BACK = HALF + 2 * PIECE
TAPS = 14
VMEM = 56 * 1024 * 1024


def place(clip, tile):
    return (clip // 2) * 2 + tile // 16, (tile // 4) % 4, tile % 4, clip % 2


def number(y, x, z, core):
    return ((y // 2) * 2 + core) * 32 + (y % 2) * 16 + x * 4 + z


def pairs(shift_of):
    out = []
    for source in range(128):
        where = place(source // 32, source % 32)
        out.append((source, number(*shift_of(*where))))
    return out


def along(core_axis, steps):
    def shift(y, x, z, core):
        if core == core_axis:
            return y, x, (z + steps) % 4, core
        return y, (x + steps) % 4, z, core

    return pairs(shift)


def along_y(steps):
    return pairs(lambda y, x, z, core: ((y + steps) % 4, x, z, core))


OTHER_CORE = pairs(lambda y, x, z, core: (y, x, z, 1 - core))


def shift_frames(tile, steps):
    if steps == 0:
        return tile
    count = tile.shape[0]
    moved = pltpu.roll(tile, count - steps, 0)
    frame = lax.broadcasted_iota(jnp.int32, tile.shape, 0) & (FRAMES - 1)
    return jnp.where(frame < FRAMES - steps, moved, 0.0)


def fill_windows(windows, rows, base):
    blank = jnp.zeros((SPAN, CH), BF16)
    for row, source in enumerate(rows):
        for time_tap in range(3):
            windows[time_tap, row, 0, pl.ds(base, SPAN)] = blank
            windows[time_tap, row, COLS + 1, pl.ds(base, SPAN)] = blank

        def column(col, carry, row=row, source=source):
            tile = source[col]
            windows[0, row, col + 1, pl.ds(base, SPAN)] = tile
            wide = tile.astype(F32)
            for time_tap in (1, 2):
                windows[time_tap, row, col + 1, pl.ds(base, SPAN)] = shift_frames(
                    wide, time_tap
                ).astype(BF16)
            return carry

        lax.fori_loop(0, COLS, column, 0)


def lanes_dot(left, right):
    return lax.dot_general(left, right, (((1,), (1,)), ((), ())), preferred_element_type=F32)


def grad_kernel(own, low, high, feats, weight, in_weight, out, windows, total, grads, spread):
    step = pl.program_id(0)

    @pl.when(step == 0)
    def _():
        fill_windows(windows, (low, own.at[0], own.at[1], high), 0)
        blank = jnp.zeros((16, CH), BF16)
        for time_tap in range(3):
            for rowout in range(4):
                for parity in range(2):
                    at = ((time_tap * 4 + rowout) * 2 + parity) * 16
                    for near in range(4):
                        for side in range(2):
                            row_tap = rowout - side
                            col_tap = parity + 2 - near
                            inside = 0 <= row_tap <= 2 and 0 <= col_tap <= 2
                            value = in_weight[time_tap, row_tap, col_tap] if inside else blank
                            spread[at : at + 16, pl.ds((near * 2 + side) * CH, CH)] = value

    for row_tap in range(3):
        left = jnp.concatenate(
            [
                windows[step, pl.ds(2 - row_tap, 2), pl.ds(2 - col_tap, COLS)].reshape(-1, CH)
                for col_tap in range(3)
            ],
            axis=1,
        )
        right = jnp.concatenate([weight[0, row_tap, col_tap] for col_tap in range(3)], axis=1)
        product = lanes_dot(left, right)
        if row_tap == 0:

            @pl.when(step == 0)
            def _():
                total[...] = product

            @pl.when(step != 0)
            def _():
                total[...] += product
        else:
            total[...] += product

    @pl.when(step == 2)
    def _():
        blank = jnp.zeros((SPAN, CH), BF16)
        for side in range(2):
            grads[side, 0, 0] = blank
            grads[side, 6, 1] = blank
            for col in range(COLS):
                values = feats[side, col].astype(F32)
                sig = jax.nn.sigmoid(values)
                slope = sig * (1.0 + values * (1.0 - sig))
                product = total[pl.ds((side * COLS + col) * SPAN, SPAN)] * slope
                grads[side, (col + 1) // 2, (col + 1) % 2] = product.astype(BF16)
        left = jnp.concatenate(
            [
                grads[side, pl.ds(near // 2, 6), near % 2].reshape(-1, CH)
                for near in range(4)
                for side in range(2)
            ],
            axis=1,
        )
        latent = lanes_dot(left, spread[...])
        for pair in range(6):
            block = latent[pair * SPAN : (pair + 1) * SPAN]
            out[:, pair * 128 : (pair + 1) * 128] = (
                block[:, 0:128]
                + shift_frames(block[:, 128:256], 1)
                + shift_frames(block[:, 256:384], 2)
            )


def input_grad(own, low, high, feats, conv_weight, in_weight):
    whole = lambda shape: pl.BlockSpec(shape, lambda i: (0,) * len(shape))
    return pl.pallas_call(
        grad_kernel,
        grid=(3,),
        in_specs=[
            whole((2, COLS, SPAN, CH)),
            whole((COLS, SPAN, CH)),
            whole((COLS, SPAN, CH)),
            whole((2, COLS, SPAN, CH)),
            pl.BlockSpec((1, 3, 3, CH, CH), lambda i: (i, 0, 0, 0, 0)),
            whole((3, 3, 3, 16, CH)),
        ],
        out_specs=whole((SPAN, 768)),
        out_shape=jax.ShapeDtypeStruct((SPAN, 768), F32),
        scratch_shapes=[
            pltpu.VMEM((3, 4, COLS + 2, SPAN, CH), BF16),
            pltpu.VMEM((2 * COLS * SPAN, CH), F32),
            pltpu.VMEM((2, 7, 2, SPAN, CH), BF16),
            pltpu.VMEM((384, 8 * CH), BF16),
        ],
        compiler_params=pltpu.CompilerParams(vmem_limit_bytes=VMEM),
        cost_estimate=pl.CostEstimate(
            flops=2 * 768 * 27 * CH * CH, bytes_accessed=12_000_000, transcendentals=768 * CH
        ),
        name="input_grad",
    )(own, low, high, feats, conv_weight, in_weight)


def weight_kernel(
    core, own, low, high, feats, own2, low2, high2, feats2, order,
    out0, out1, out2, out3, windows, active, turned,
):
    step = pl.program_id(0)

    @pl.when(step == 0)
    def _():
        fill_windows(windows, (low, own.at[0], own.at[1], high), 0)
        fill_windows(windows, (low2, own2.at[0], own2.at[1], high2), SPAN)
        for base, source in ((0, feats), (SPAN, feats2)):
            for side in range(2):

                def column(col, carry, base=base, source=source, side=side):
                    values = source[side, col].astype(F32)
                    active[side, col, pl.ds(base, SPAN)] = jax.nn.silu(values).astype(BF16)
                    return carry

                lax.fori_loop(0, COLS, column, 0)
        turned[...] = lanes_dot(order[...], active[...].reshape(-1, CH)).astype(BF16)

    first = core[0] * (TAPS - 1) + 2 * step

    def window(tap):
        time_tap = lax.div(tap, 9)
        rest = tap - 9 * time_tap
        row_tap = lax.div(rest, 3)
        col_tap = rest - 3 * row_tap
        return windows[time_tap, pl.ds(2 - row_tap, 2), pl.ds(2 - col_tap, COLS)].reshape(-1, CH)

    right = jnp.concatenate([window(first), window(first + 1)], axis=1)
    product = jnp.dot(turned[...], right, preferred_element_type=F32).astype(BF16)
    for part, out in enumerate((out0, out1, out2, out3)):
        for which in range(2):
            out[which] = product[part * 96 : (part + 1) * 96, which * CH : (which + 1) * CH]


def weight_grad(core, own, low, high, feats, own2, low2, high2, feats2, order):
    whole = lambda shape: pl.BlockSpec(shape, lambda i: (0,) * len(shape))
    rows = [whole((2, COLS, SPAN, CH)), whole((COLS, SPAN, CH)), whole((COLS, SPAN, CH)),
            whole((2, COLS, SPAN, CH))]
    return pl.pallas_call(
        weight_kernel,
        grid=(TAPS // 2,),
        in_specs=[pl.BlockSpec(memory_space=pltpu.SMEM), *rows, *rows, whole((CH, CH))],
        out_specs=[pl.BlockSpec((2, 96, CH), lambda i: (i, 0, 0))] * 4,
        out_shape=[jax.ShapeDtypeStruct((TAPS, 96, CH), BF16)] * 4,
        scratch_shapes=[
            pltpu.VMEM((3, 4, COLS + 2, 2 * SPAN, CH), BF16),
            pltpu.VMEM((2, COLS, 2 * SPAN, CH), BF16),
            pltpu.VMEM((CH, 2 * COLS * 2 * SPAN), BF16),
        ],
        compiler_params=pltpu.CompilerParams(vmem_limit_bytes=VMEM),
        cost_estimate=pl.CostEstimate(
            flops=2 * 1536 * TAPS * CH * CH, bytes_accessed=12_000_000, transcendentals=1536 * CH
        ),
        name="weight_grad",
    )(core, own, low, high, feats, own2, low2, high2, feats2, order)


def stats_kernel(states, mods, head_input, mean, inv):
    values = states[...].astype(F32)
    average = jnp.mean(values, axis=-1, keepdims=True)
    centered = values - average
    inv_std = lax.rsqrt(jnp.mean(centered * centered, axis=-1, keepdims=True) + 1e-06)
    head_input[...] = (centered * inv_std * (1.0 + mods[1:2, :]) + mods[0:1, :]).astype(BF16)
    mean[...] = jnp.broadcast_to(average, mean.shape)
    inv[...] = jnp.broadcast_to(inv_std, inv.shape)


def stats(states, mods):
    tokens = states.shape[0]
    return pl.pallas_call(
        stats_kernel,
        grid=(tokens // 32,),
        in_specs=[
            pl.BlockSpec((32, WIDTH), lambda i: (i, 0)),
            pl.BlockSpec((2, WIDTH), lambda i: (0, 0)),
        ],
        out_specs=[
            pl.BlockSpec((32, WIDTH), lambda i: (i, 0)),
            pl.BlockSpec((32, 128), lambda i: (i, 0)),
            pl.BlockSpec((32, 128), lambda i: (i, 0)),
        ],
        out_shape=[
            jax.ShapeDtypeStruct((tokens, WIDTH), BF16),
            jax.ShapeDtypeStruct((tokens, 128), F32),
            jax.ShapeDtypeStruct((tokens, 128), F32),
        ],
        compiler_params=pltpu.CompilerParams(vmem_limit_bytes=VMEM),
        cost_estimate=pl.CostEstimate(
            flops=10_000_000, bytes_accessed=4_000_000, transcendentals=192
        ),
        name="token_stats",
    )(states, mods)


def head_kernel(
    sent, states, head_input, head_weight, mods, mean, inv,
    load, patch_out, sum_out, dot_out, patch, patch_t, gains, piece, sums, dots,
):
    step = pl.program_id(0)
    tokens = patch.shape[0]

    @pl.when(step == 0)
    def _():
        below = lax.broadcasted_iota(jnp.int32, (SPAN, 128), 0)
        lane = lax.broadcasted_iota(jnp.int32, (SPAN, 128), 1)
        parts = []
        for pair in range(6):
            here = sent[:, pair * 128 : (pair + 1) * 128]
            swapped = pltpu.roll(here, 64, 1)
            before = jnp.where(below > 0, pltpu.roll(swapped, 1, 0), 0.0)
            after = jnp.where(below < SPAN - 1, pltpu.roll(swapped, SPAN - 1, 0), 0.0)
            summed = here + jnp.where(lane < 64, before, after)
            inside = (lane >= 32) & (lane < 96)
            parts.append(jnp.where(inside, summed, 0.0).astype(BF16))
        stacked = jnp.concatenate(parts, axis=0)
        token = lax.broadcasted_iota(jnp.int32, (tokens, tokens), 0)
        source = lax.broadcasted_iota(jnp.int32, (tokens, tokens), 1)
        match = (source & (SPAN - 1)) * 6 + lax.shift_right_logical(source, 5) == token
        pick = jnp.where(match, 1.0, 0.0).astype(BF16)
        ordered = jnp.dot(pick, stacked, preferred_element_type=F32)
        patch[...] = ordered.astype(BF16)
        patch_out[...] = ordered.astype(BF16)
        patch_t[...] = ordered.T.astype(BF16)
        sums[...] = jnp.zeros_like(sums)
        dots[...] = jnp.zeros_like(dots)
        piece[...] = jnp.zeros_like(piece)

    grad = lanes_dot(patch[...], head_weight[...])
    normed = (states[...].astype(F32) - mean[:, 0:1]) * inv[:, 0:1]
    weighted = grad * normed
    at = pl.multiple_of(step * STEP, STEP)
    gains[0:1, pl.ds(at, STEP)] = jnp.sum(grad, axis=0, keepdims=True)
    gains[1:2, pl.ds(at, STEP)] = jnp.sum(weighted, axis=0, keepdims=True)
    scale = 1.0 + mods[1:2, :]
    sums[...] += jnp.sum(grad * scale, axis=-1, keepdims=True)
    dots[...] += jnp.sum(weighted * scale, axis=-1, keepdims=True)
    product = jnp.dot(patch_t[...], head_input[...], preferred_element_type=F32)
    half = lax.div(step, 5)
    lanes = pl.multiple_of((step - 5 * half) * STEP, STEP)
    load[pl.ds(pl.multiple_of(half * 64, 64), 64), pl.ds(lanes, STEP)] = product[32:96].astype(BF16)

    @pl.when(step == pl.num_programs(0) - 1)
    def _():
        for block in range(80):
            row, lane = divmod(block, 40)
            piece[block // 3 : block // 3 + 1, pl.ds((block % 3) * 128, 128)] = gains[
                row : row + 1, lane * 128 : (lane + 1) * 128
            ]
        narrow = piece[...].astype(BF16)
        for group in range(4):
            load[group * 32 : (group + 1) * 32, HALF:LOAD] = narrow
        sum_out[...] = sums[...] * (1.0 / WIDTH)
        dot_out[...] = dots[...] * (1.0 / WIDTH)


def head_sums(sent, states, head_input, head_weight, mods, mean, inv):
    tokens = states.shape[0]
    fixed = lambda shape: pl.BlockSpec(shape, lambda i: (0, 0))
    return pl.pallas_call(
        head_kernel,
        grid=(WIDTH // STEP,),
        in_specs=[
            fixed((SPAN, 768)),
            pl.BlockSpec((tokens, STEP), lambda i: (0, i)),
            pl.BlockSpec((tokens, STEP), lambda i: (0, i)),
            pl.BlockSpec((STEP, 128), lambda i: (i, 0)),
            pl.BlockSpec((2, STEP), lambda i: (0, i)),
            fixed((tokens, 128)),
            fixed((tokens, 128)),
        ],
        out_specs=[fixed((128, LOAD)), fixed((tokens, 128)), fixed((tokens, 128)),
                   fixed((tokens, 128))],
        out_shape=[
            jax.ShapeDtypeStruct((128, LOAD), BF16),
            jax.ShapeDtypeStruct((tokens, 128), BF16),
            jax.ShapeDtypeStruct((tokens, 128), F32),
            jax.ShapeDtypeStruct((tokens, 128), F32),
        ],
        scratch_shapes=[
            pltpu.VMEM((tokens, 128), BF16),
            pltpu.VMEM((128, tokens), BF16),
            pltpu.VMEM((2, WIDTH), F32),
            pltpu.VMEM((32, PIECE), F32),
            pltpu.VMEM((tokens, 128), F32),
            pltpu.VMEM((tokens, 128), F32),
        ],
        compiler_params=pltpu.CompilerParams(vmem_limit_bytes=VMEM),
        cost_estimate=pl.CostEstimate(
            flops=2 * 2 * 192 * 128 * WIDTH, bytes_accessed=7_000_000, transcendentals=0
        ),
        name="head_sums",
    )(sent, states, head_input, head_weight, mods, mean, inv)


def hidden_kernel(patch, states, head_weight, mods, mean, inv, sums, dots, out):
    grad = lanes_dot(patch[...], head_weight[...])
    inv_std = inv[:, 0:1]
    normed = (states[...].astype(F32) - mean[:, 0:1]) * inv_std
    scaled = grad * (1.0 + mods[1:2, :])
    out[...] = ((scaled - sums[:, 0:1] - normed * dots[:, 0:1]) * inv_std).astype(BF16)


def hidden_grads(patch, states, head_weight, mods, mean, inv, sums, dots):
    tokens = states.shape[0]
    fixed = lambda shape: pl.BlockSpec(shape, lambda i: (0, 0))
    return pl.pallas_call(
        hidden_kernel,
        grid=(WIDTH // STEP,),
        in_specs=[
            fixed((tokens, 128)),
            pl.BlockSpec((tokens, STEP), lambda i: (0, i)),
            pl.BlockSpec((STEP, 128), lambda i: (i, 0)),
            pl.BlockSpec((2, STEP), lambda i: (0, i)),
            *[fixed((tokens, 128))] * 4,
        ],
        out_specs=pl.BlockSpec((tokens, STEP), lambda i: (0, i)),
        out_shape=jax.ShapeDtypeStruct((tokens, WIDTH), BF16),
        compiler_params=pltpu.CompilerParams(vmem_limit_bytes=VMEM),
        cost_estimate=pl.CostEstimate(
            flops=2 * 192 * 128 * WIDTH, bytes_accessed=6_000_000, transcendentals=0
        ),
        name="hidden_grads",
    )(patch, states, head_weight, mods, mean, inv, sums, dots)


def channel_order(core, x, z, y_low):
    at = jnp.arange(CH, dtype=jnp.int32)
    first, second, rel, inner = at // 96, (at // 24) % 4, (at // 12) % 2, at % 12
    x_at = (x + jnp.where(core == 0, second, first)) % 4
    z_at = (z + jnp.where(core == 0, first, second)) % 4
    channel = 12 * ((y_low ^ rel) * 16 + x_at * 4 + z_at) + inner
    return (channel[:, None] == jnp.arange(CH, dtype=jnp.int32)[None, :]).astype(BF16)


def added(*terms):
    return functools.reduce(lambda a, b: a + b, [term.astype(F32) for term in terms])


def reduce_weights(parts):
    got = [lax.ppermute(parts[k], BOTH, along(0, k)) for k in (1, 2, 3)]
    summed = added(parts[0], *got).astype(BF16)
    rows = [summed[:, 24 * k : 24 * (k + 1)] for k in range(4)]
    got = [lax.ppermute(rows[k], BOTH, along(1, k)) for k in (1, 2, 3)]
    summed = added(rows[0], *got).astype(BF16)
    same, flipped = summed[:, :12], summed[:, 12:]
    far = lax.ppermute(same, BOTH, along_y(2))
    up = lax.ppermute(flipped, BOTH, along_y(1))
    down = lax.ppermute(flipped, BOTH, along_y(3))
    return added(same, far) + added(up, down)


def local(
    features, pixel_grad, frame_list, conv_weight, in_weight, last_hidden, modulation, head_weight
):
    clips, frames, rows_here, columns, _ = features.shape
    clip = lax.axis_index("clip")
    tile = lax.axis_index("tile")
    _, x, z, core = place(clip, tile)
    y_low = tile // 16

    scored = jnp.any(
        frame_list[:, None, :] == jnp.arange(frames, dtype=jnp.int32)[None, :, None], axis=-1
    )
    masked = pixel_grad * scored.astype(BF16)[:, :, None, None, None]
    own = jnp.transpose(masked, (2, 3, 0, 1, 4)).reshape(rows_here, columns, SPAN, CH)
    feats = jnp.transpose(features, (2, 3, 0, 1, 4)).reshape(rows_here, columns, SPAN, CH)

    up = [(i, i + 1) for i in range(31)]
    down = [(i + 1, i) for i in range(31)]
    low = lax.ppermute(own[1], "tile", up)
    high = lax.ppermute(own[0], "tile", down)
    own2 = lax.ppermute(own, BOTH, OTHER_CORE)
    feats2 = lax.ppermute(feats, BOTH, OTHER_CORE)
    low2 = lax.ppermute(low, BOTH, OTHER_CORE)
    high2 = lax.ppermute(high, BOTH, OTHER_CORE)

    mods = lax.dynamic_index_in_dim(modulation, y_low, 0, keepdims=False)
    head_wide = jnp.pad(head_weight, ((0, 0), (32, 32)))
    head_input, mean, inv = stats(last_hidden, mods)

    sent = input_grad(own, low, high, feats, conv_weight, in_weight)
    parts = weight_grad(
        core.astype(jnp.int32).reshape(1), own, low, high, feats, own2, low2, high2, feats2,
        channel_order(core, x, z, y_low),
    )
    sent = lax.all_to_all(sent, "tile", 0, 0, tiled=True)
    load, patch, sums, dots = head_sums(
        sent, last_hidden, head_input, head_wide, mods, mean, inv
    )
    got = lax.all_to_all(load, BOTH, 0, 0, tiled=True)
    hidden_grad = hidden_grads(patch, last_hidden, head_wide, mods, mean, inv, sums, dots)

    line = jnp.sum(got[:, :HALF].astype(F32), axis=0)
    mine = lax.dynamic_slice_in_dim(got[:, HALF:], clip * 32, 32, 0).astype(F32)
    gains = jnp.sum(mine.reshape(2, 16, PIECE), axis=1).reshape(-1)
    line = jnp.concatenate([line, gains]).astype(BF16)
    back = lax.all_to_all(
        jnp.broadcast_to(line[None], (128, BACK)), BOTH, 0, 0, tiled=True
    )
    head_weight_grad = (
        jnp.transpose(back[:, :HALF].reshape(2, 64, HALF), (0, 2, 1))
        .reshape(WIDTH, 64)
        .astype(F32)
    )
    gains = lax.dynamic_slice_in_dim(back[:, HALF:], clip * 32, 32, 0).astype(F32)
    modulation_grad = (
        jnp.transpose(gains.reshape(32, 2, PIECE), (1, 0, 2))
        .reshape(2, 32 * PIECE)[:, : 2 * WIDTH]
        .reshape(2, 2, WIDTH)
    )

    share = reduce_weights(parts)
    theirs = lax.ppermute(share, BOTH, OTHER_CORE)
    conv_weight_grad = jnp.where(
        core == 0,
        jnp.concatenate([share, theirs[1:]], axis=0),
        jnp.concatenate([theirs, share[1:]], axis=0),
    ).reshape(3, 3, 3, 12, CH)
    return (hidden_grad, head_weight_grad, modulation_grad, conv_weight_grad)


def solution(mesh):
    return jax.shard_map(
        local,
        mesh=mesh,
        in_specs=(
            P("clip", None, "tile", None, None),
            P("clip", None, "tile", None, None),
            P("clip", None),
            P(),
            P(),
            P(("clip", "tile"), None),
            P("clip", None, None),
            P(),
        ),
        out_specs=(
            P(("clip", "tile"), None),
            P(),
            P("clip", None, None),
            P(None, None, None, "tile", None),
        ),
        check_vma=False,
    )
```

time: 966 us -> 165 us (0.17)
  waiting for transfers between devices: 582 us -> 31.9 us
  matrix products: 182 us -> 0 us
  local copies, waits for them, and re-layouts: 129 us -> 14.6 us
  Pallas kernels: 0 us -> 53.3 us
  starting transfers between devices: 28.3 us -> 46.9 us
  between operations: 15 us -> 1 us
    psum x3 -> x0, waiting for transfers between devices: 576 us -> none  [the longest x1 377 us: local(): modulation_grad = lax.psum(clip_terms, 'tile')]
    dot_general x84 -> x0, matrix products: 182 us -> none  [the longest x54 130 us: conv_back(): jnp.dot(window.reshape(-1, window.shape[-1]), weight[time_tap, row_tap, c...]
    reshape x57 -> x2, local copies, waits for them, and re-layouts: 101 us -> 0.75 us  [the longest x1 0.73 us: local(): modulation_grad = jnp.transpose(gains.reshape(32, 2, PIECE), (1, 0, 2)).r...]
    pallas_call x0 -> x5, Pallas kernels: none -> 53.3 us  [the longest x1 15.7 us: input_grad(): pl.pallas_call(grad_kernel, grid=(3,), in_specs=[whole((2, COLS, SPAN, CH...]
    slice x8 -> x10, local copies, waits for them, and re-layouts: 18.8 us -> 1.14 us  [the longest x2 0.86 us: local(): high = lax.ppermute(own[0], 'tile', down)]
    ppermute x4 -> x16, waiting for transfers between devices: 0.03 us -> 15.9 us  [the longest x1 7.12 us: reduce_weights(): far = lax.ppermute(same, BOTH, along_y(2))]
    ppermute x4 -> x16, starting transfers between devices: 13.5 us -> 24.6 us  [the longest x1 5.22 us: local(): low = lax.ppermute(own[1], 'tile', up)]
    all_to_all x1 -> x3, waiting for transfers between devices: 5.4 us -> 16 us  [the longest x1 16 us: local(): got = lax.all_to_all(load, BOTH, 0, 0, tiled=True)]
  transfers between devices with their start and end apart: 8 -> 19, of which waited for: 4 -> 7; matrix products, arithmetic and copies ran while one was open for 7% -> 15% of each run, Pallas kernels for 0% -> 24%
where the time goes in v1:
time: 165 us; the launch traced here: 164 us
  Pallas kernels  53.3 us (32%)
  starting transfers between devices  46.9 us (28%)
  waiting for transfers between devices  31.9 us (19%)
  other arithmetic  16.2 us (10%)
  local copies, waits for them, and re-layouts  14.6 us (9%)
    all_to_all x1, waiting for transfers between devices, local(): got = lax.all_to_all(load, BOTH, 0, 0, tiled=True)  16 us
    pallas_call x1, Pallas kernels, input_grad(): pl.pallas_call(grad_kernel, grid=(3,), in_specs=[whole((2, COLS, SPAN, CH...  15.7 us
    pallas_call x1, Pallas kernels, weight_grad(): pl.pallas_call(weight_kernel, grid=(TAPS // 2,), in_specs=[pl.BlockSpec(m...  14.1 us
    all_to_all x1, starting transfers between devices, local(): sent = lax.all_to_all(sent, 'tile', 0, 0, tiled=True)  9.51 us
    pallas_call x1, Pallas kernels, head_sums(): pl.pallas_call(head_kernel, grid=(WIDTH // STEP,), in_specs=[fixed((SPAN,...  9.31 us
    pallas_call x1, Pallas kernels, hidden_grads(): pl.pallas_call(hidden_kernel, grid=(WIDTH // STEP,), in_specs=[fixed((tok...  8.32 us
    all_to_all x1, starting transfers between devices, local(): got = lax.all_to_all(load, BOTH, 0, 0, tiled=True)  7.94 us
    ppermute x1, waiting for transfers between devices, reduce_weights(): far = lax.ppermute(same, BOTH, along_y(2))  7.12 us
  transfers between devices with their start and end apart: 19, of which 7 were waited for; matrix products, arithmetic and copies ran while one was open for 15% of the time, Pallas kernels for 24%

profile of v1, /device:TPU:1, one launch (start us, length us, event | category | flops | bytes accessed | tf_op | source)
XLA Modules:
  0.0 163.9 jit_solution(16124597741884077753)
XLA Ops:
  0.6 0.0 copy-start
  0.6 0.8 fusion.1
  1.5 1.7 %multiply_bitcast_fusion = bf16[2,12,2,16,384]{4,0,1,3,2:T(2,128)(2,1)S(1)} fusion(bf16[2,16,2,12,384]{4,2,3,1,0:T(2,128)(2,1)} %param.9, bf16[2,16]{1,0:T(2,128)(2,1)S(1)} %convert_element_type.76), kind=kLoop, calls=%fused_computation.7 | loop fusion | flops 294912 | bytes 1179712 | tf_op jit(solution)/shard_map/transpose | solution.py:459
  3.1 0.8 fusion.24
  4.0 0.0 copy-start.3
  4.0 5.2 %collective-permute-start = (bf16[12,32,384]{2,1,0:T(8,128)(2,1)S(1)}, bf16[12,32,384]{2,1,0:T(8,128)(2,1)}, u32[]{:S(2)}, u32[]{:S(2)}) collective-permute-start(bf16[12,32,384]{2,1,0:T(8,128)(2,1)S(1)} %bitcast.50), channel_id=1, source_target_pairs={{0,1},{1,2},{2,3},{3,4},{4,5},{5,6},{6,7},{7,8},{8,9},{9,10},{10,1... | collective-permute-start | bytes 884744 | tf_op jit(solution)/shard_map/ppermute | solution.py:464
  9.3 1.3 collective-permute-start.1
  10.6 0.1 copy.44
  10.7 0.0 copy-start.4
  10.7 1.0 collective-permute-start.2
  11.7 0.1 copy.47
  11.8 0.1 collective-permute-start.5
  11.9 0.7 dynamic-slice_bitcast_fusion.mods
  12.7 1.5 collective-permute-done.low
  14.2 1.5 collective-permute-start.3
  15.8 3.1 %collective-permute-done.1.high = bf16[12,32,384]{2,1,0:T(8,128)(2,1)} collective-permute-done((bf16[12,32,384]{2,1,0:T(8,128)(2,1)S(1)}, bf16[12,32,384]{2,1,0:T(8,128)(2,1)}, u32[]{:S(2)}, u32[]{:S(2)}) %collective-permute-start.1) | collective-permute-done | bytes 294944 | tf_op jit(solution)/shard_map/ppermute | solution.py:465
  18.9 1.9 %collective-permute-start.4 = (bf16[12,32,384]{2,1,0:T(8,128)(2,1)}, bf16[12,32,384]{2,1,0:T(8,128)(2,1)}, u32[]{:S(2)}, u32[]{:S(2)}) collective-permute-start(bf16[12,32,384]{2,1,0:T(8,128)(2,1)} %collective-permute-done.1.high), channel_id=1, source_target_pairs={{0,32},{1,33},{2,34},{3,35},{4,36},{5,37},{6,38},{7,39},{8,40},{9,... | collective-permute-start | bytes 884744 | tf_op jit(solution)/shard_map/ppermute | solution.py:469
  20.7 15.7 %input_grad.1 = f32[32,768]{1,0:T(8,128)} custom-call(bf16[2,12,32,384]{3,2,1,0:T(8,128)(2,1)} %bitcast.43, bf16[12,32,384]{2,1,0:T(8,128)(2,1)} %collective-permute-done.low, bf16[12,32,384]{2,1,0:T(8,128)(2,1)} %collective-permute-done.1.high, bf16[2,12,32,384]{3,2,1,0:T(8,128)(2,1)} %bitcast.46, bf16[3,3,3,384,384]{4,3,2,1,0:T(8,128)(2,1)} %weight.1, ...), custom_call_target="tpu_custom_call" | custom-call | flops 6115295232 | bytes 12000000 | tf_op jit(solution)/shard_map/input_grad/pallas_call | solution.py:165
  36.4 1.6 copy.48
  38.1 9.5 %all-to-all-start = ((f32[32,1,768]{2,1,0:T(1,128)}), f32[32,1,768]{2,1,0:T(1,128)S(1)}, u32[]{:S(2)}, u32[]{:S(2)}) async-start(f32[32,1,768]{2,1,0:T(1,128)} %copy.48), calls=%async_computation | async-start | bytes 196608 | tf_op jit(solution)/shard_map/all_to_all | solution.py:480
  47.6 0.8 fusion.order
  48.4 0.7 copy.49
  49.2 1.5 pad.4.head_weight
  50.7 5.8 %token_stats.1 = (bf16[192,5120]{1,0:T(8,128)(2,1)}, f32[192,128]{1,0:T(8,128)}, f32[192,128]{1,0:T(8,128)}) custom-call(bf16[192,5120]{1,0:T(8,128)(2,1)} %states.5, f32[2,5120]{1,0:T(2,128)} %dynamic-slice_bitcast_fusion.mods), custom_call_target="tpu_custom_call" | custom-call | flops 10000000 | bytes 4000000 | tf_op jit(solution)/shard_map/token_stats/pallas_call | solution.py:264
  56.5 0.7 copy.61
  57.2 14.1 %weight_grad.1 = (bf16[14,96,384]{2,1,0:T(8,128)(2,1)}, bf16[14,96,384]{2,1,0:T(8,128)(2,1)}, bf16[14,96,384]{2,1,0:T(8,128)(2,1)}, bf16[14,96,384]{2,1,0:T(8,128)(2,1)}) custom-call(s32[1]{0:T(128)} %bitcast.14.core, bf16[2,12,32,384]{3,2,1,0:T(8,128)(2,1)} %bitcast.44, bf16[12,32,384]{2,1,0:T(8,128)(2,1)} %collective-permute-done.low, ...), custom_call_target="tpu_custom_call" | custom-call | flops 6341787648 | bytes 12000000 | tf_op jit(solution)/shard_map/weight_grad/pallas_call | solution.py:233
  71.3 1.2 collective-permute-start.6
  72.6 2.4 %collective-permute-start.7 = (bf16[14,96,384]{2,1,0:T(8,128)(2,1)}, bf16[14,96,384]{2,1,0:T(8,128)(2,1)}, u32[]{:S(2)}, u32[]{:S(2)}) collective-permute-start(bf16[14,96,384]{2,1,0:T(8,128)(2,1)} %get-tuple-element.24), channel_id=1, source_target_pairs={{0,2},{1,3},{2,0},{3,1},{4,6},{5,7},{6,4},{7,5},{8,10},{9,11},{10,... | collective-permute-start | bytes 3096584 | tf_op jit(solution)/shard_map/ppermute | solution.py:434
  75.0 1.2 collective-permute-start.8
  76.2 9.3 %head_sums.1 = (bf16[128,2944]{1,0:T(8,128)(2,1)}, bf16[192,128]{1,0:T(8,128)(2,1)}, f32[192,128]{1,0:T(8,128)}, f32[192,128]{1,0:T(8,128)}) custom-call(f32[32,768]{1,0:T(8,128)} %bitcast.48, bf16[192,5120]{1,0:T(8,128)(2,1)} %states.5, bf16[192,5120]{1,0:T(8,128)(2,1)} %get-tuple-element.15.head_input, bf16[5120,128]{1,0:T(8,128)(2,1)} %pad.4.head_weight, ...), custom_call_target="tpu_custom_call" | custom-call | flops 503316480 | bytes 7000000 | tf_op jit(solution)/shard_map/head_sums/pallas_call | solution.py:353
  85.5 0.5 broadcast.204
  86.0 2.2 %reduce.4 = bf16[128,2944]{1,0:T(8,128)(2,1)S(1)} reduce(bf16[128,1,2944]{2,0,1:T(8,128)(2,1)} %bitcast.39, bf16[]{:T(256)} %broadcast.204), dimensions={1}, to_apply=%copy.50.reduce_sub_computation | reduce | bytes 1507330 | tf_op jit(solution)/shard_map/all_to_all | solution.py:484
  88.3 1.7 %reshape.186 = bf16[128,2,1472]{2,1,0:T(2,128)(2,1)} reshape(bf16[128,2944]{1,0:T(8,128)(2,1)S(1)} %reduce.4) | data formatting | bytes 1507328
  89.9 7.9 %all-to-all-start.1 = ((bf16[128,2,1472]{2,1,0:T(2,128)(2,1)}), bf16[128,2,1472]{2,1,0:T(2,128)(2,1)S(1)}, u32[]{:S(2)}, u32[]{:S(2)}) async-start(bf16[128,2,1472]{2,1,0:T(2,128)(2,1)} %reshape.186), calls=%async_computation.1 | async-start | bytes 1572864 | tf_op jit(solution)/shard_map/all_to_all | solution.py:484
  97.9 16.0 %all-to-all-done.1 = bf16[128,2,1472]{2,1,0:T(2,128)(2,1)S(1)} async-done(((bf16[128,2,1472]{2,1,0:T(2,128)(2,1)}), bf16[128,2,1472]{2,1,0:T(2,128)(2,1)S(1)}, u32[]{:S(2)}, u32[]{:S(2)}) %all-to-all-start.1) | async-done | bytes 753696 | tf_op jit(solution)/shard_map/all_to_all | solution.py:484
  113.8 1.0 reshape.187
  114.9 0.1 copy.60
  115.0 0.1 slice_reduce_fusion
  115.2 0.9 broadcast_in_dim.2
  116.1 5.8 %reduce.5 = bf16[128,3328]{1,0:T(8,128)(2,1)S(1)} reduce(bf16[128,1,3328]{2,1,0:T(2,128)(2,1)S(1)} %broadcast_in_dim.2, bf16[]{:T(256)} %broadcast.204), dimensions={1}, to_apply=%broadcast_in_dim.2.reduce_sub_computation | reduce | bytes 1703938 | tf_op jit(solution)/shard_map/broadcast_in_dim | solution.py:492
  121.9 1.1 reshape.188
  123.0 4.8 %all-to-all-start.2 = ((bf16[128,2,1664]{2,1,0:T(2,128)(2,1)}), bf16[128,2,1664]{2,1,0:T(2,128)(2,1)S(1)}, u32[]{:S(2)}, u32[]{:S(2)}) async-start(bf16[128,2,1664]{2,1,0:T(2,128)(2,1)} %reshape.188), calls=%async_computation.2 | async-start | bytes 1703936 | tf_op jit(solution)/shard_map/all_to_all | solution.py:491
  127.9 2.4 %add_convert_fusion = bf16[14,96,384]{2,1,0:T(8,128)(2,1)S(1)} fusion(bf16[14,96,384]{2,1,0:T(8,128)(2,1)} %collective-permute-done.8, bf16[14,96,384]{2,1,0:T(8,128)(2,1)} %collective-permute-done.7, bf16[14,96,384]{2,1,0:T(8,128)(2,1)} %collective-permute-done.6, bf16[14,96,384]{2,1,0:T(8,128)(2,1)S(1)} %copy-done.1), kind=kLoop, calls=%fused_computation | loop fusion | flops 4128768 | bytes 5160960 | tf_op jit(solution)/shard_map/convert_element_type | solution.py:435
  130.2 0.1 fusion.23
  130.3 3.5 %collective-permute-start.10 = (bf16[14,24,384]{2,1,0:T(8,128)(2,1)S(1)}, bf16[14,24,384]{2,1,0:T(8,128)(2,1)S(1)}, u32[]{:S(2)}, u32[]{:S(2)}) collective-permute-start(bf16[14,24,384]{2,1,0:T(8,128)(2,1)S(1)} %get-tuple-element.28), channel_id=1, source_target_pairs={{0,8},{1,9},{2,10},{3,11},{4,12},{5,13},{6,14},{7,15},{8,0},{9,1},... | collective-permute-start | bytes 774152 | tf_op jit(solution)/shard_map/ppermute | solution.py:437
  133.8 0.6 collective-permute-start.11
  134.4 0.8 collective-permute-start.9
  135.3 8.3 %hidden_grads.1 = bf16[192,5120]{1,0:T(8,128)(2,1)} custom-call(bf16[192,128]{1,0:T(8,128)(2,1)} %get-tuple-element.18.patch, bf16[192,5120]{1,0:T(8,128)(2,1)} %states.5, bf16[5120,128]{1,0:T(8,128)(2,1)} %pad.4.head_weight, f32[2,5120]{1,0:T(2,128)} %dynamic-slice_bitcast_fusion.mods, f32[192,128]{1,0:T(8,128)} %get-tuple-element.16.mean, ...), custom_call_target="tpu_custom_call" | custom-call | flops 251658240 | bytes 6000000 | tf_op jit(solution)/shard_map/hidden_grads/pallas_call | solution.py:400
  143.6 1.5 collective-permute-done.10
  145.1 0.9 collective-permute-done.11
  146.0 1.8 %collective-permute-done.9 = bf16[14,24,384]{2,1,0:T(8,128)(2,1)S(1)} collective-permute-done((bf16[14,24,384]{2,1,0:T(8,128)(2,1)S(1)}, bf16[14,24,384]{2,1,0:T(8,128)(2,1)S(1)}, u32[]{:S(2)}, u32[]{:S(2)}) %collective-permute-start.9) | collective-permute-done | bytes 258080 | tf_op jit(solution)/shard_map/ppermute | solution.py:437
  147.7 0.1 add_convert_fusion.1
  147.9 0.5 collective-permute-start.13
  148.4 2.3 %collective-permute-start.14 = (bf16[14,12,384]{2,1,0:T(8,128)(2,1)S(1)}, bf16[14,12,384]{2,1,0:T(8,128)(2,1)}, u32[]{:S(2)}, u32[]{:S(2)}) collective-permute-start(bf16[14,12,384]{2,1,0:T(8,128)(2,1)S(1)} %get-tuple-element.32), channel_id=1, source_target_pairs={{0,80},{1,81},{2,82},{3,83},{4,84},{5,85},{6,86},{7,87},{8,88},{9,... | collective-permute-start | bytes 387080 | tf_op jit(solution)/shard_map/ppermute | solution.py:442
  150.7 0.5 collective-permute-start.12
  151.2 0.7 reshape.189
  151.9 0.1 copy.59
  152.1 7.1 %collective-permute-done.12 = bf16[14,12,384]{2,1,0:T(8,128)(2,1)} collective-permute-done((bf16[14,12,384]{2,1,0:T(8,128)(2,1)S(1)}, bf16[14,12,384]{2,1,0:T(8,128)(2,1)}, u32[]{:S(2)}, u32[]{:S(2)}) %collective-permute-start.12) | collective-permute-done | bytes 129056 | tf_op jit(solution)/shard_map/ppermute | solution.py:440
  159.2 1.1 add_add_fusion
  160.3 0.5 collective-permute-start.15
  160.9 0.1 convert_bitcast_fusion
  161.0 1.1 copy.55
  162.1 0.7 reshape.183
  162.9 0.9 maximum_select_fusion
  (37 shorter events, 0.5 us)
Async XLA Ops:
  0.6 11.3 %copy-start = (f32[2,2,5120]{2,1,0:T(2,128)S(1)}, f32[2,2,5120]{2,1,0:T(2,128)}, u32[]{:S(2)}) copy-start(f32[2,2,5120]{2,1,0:T(2,128)} %param.14) | copy-start | bytes 245764
  4.0 7.8 %copy-start.3 = (bf16[2,16,2,12,384]{4,2,3,1,0:T(2,128)(2,1)S(1)}, bf16[2,16,2,12,384]{4,2,3,1,0:T(2,128)(2,1)}, u32[]{:S(2)}) copy-start(bf16[2,16,2,12,384]{4,2,3,1,0:T(2,128)(2,1)} %param.8) | copy-start | bytes 1769476
  4.0 10.2 %collective-permute-start = (bf16[12,32,384]{2,1,0:T(8,128)(2,1)S(1)}, bf16[12,32,384]{2,1,0:T(8,128)(2,1)}, u32[]{:S(2)}, u32[]{:S(2)}) collective-permute-start(bf16[12,32,384]{2,1,0:T(8,128)(2,1)S(1)} %bitcast.50), channel_id=1, source_target_pairs={{0,1},{1,2},{2,3},{3,4},{4,5},{5,6},{6,7},{7,8},{8,9},{9,10},{10,1... | collective-permute-start | bytes 884744 | tf_op jit(solution)/shard_map/ppermute | solution.py:464
  9.3 9.6 %collective-permute-start.1 = (bf16[12,32,384]{2,1,0:T(8,128)(2,1)S(1)}, bf16[12,32,384]{2,1,0:T(8,128)(2,1)}, u32[]{:S(2)}, u32[]{:S(2)}) collective-permute-start(bf16[12,32,384]{2,1,0:T(8,128)(2,1)S(1)} %bitcast.49), channel_id=1, source_target_pairs={{1,0},{2,1},{3,2},{4,3},{5,4},{6,5},{7,6},{8,7},{9,8},{10,9},{11,1... | collective-permute-start | bytes 884744 | tf_op jit(solution)/shard_map/ppermute | solution.py:465
  10.7 10.0 %copy-start.4 = (bf16[2,12,2,16,384]{4,3,2,1,0:T(8,128)(2,1)}, bf16[2,12,2,16,384]{4,3,2,1,0:T(8,128)(2,1)S(1)}, u32[]{:S(2)}) copy-start(bf16[2,12,2,16,384]{4,3,2,1,0:T(8,128)(2,1)S(1)} %copy.44) | copy-start | bytes 1769476
  10.7 46.5 %collective-permute-start.2 = (bf16[2,12,32,384]{3,2,1,0:T(8,128)(2,1)S(1)}, bf16[2,12,32,384]{3,2,1,0:T(8,128)(2,1)}, u32[]{:S(2)}, u32[]{:S(2)}) collective-permute-start(bf16[2,12,32,384]{3,2,1,0:T(8,128)(2,1)S(1)} %bitcast.42), channel_id=1, source_target_pairs={{0,32},{1,33},{2,34},{3,35},{4,36},{5,37},{6,38},{7,39},{8,40},{9,... | collective-permute-start | bytes 1769480 | tf_op jit(solution)/shard_map/ppermute | solution.py:466
  11.8 8.9 %copy-start.5 = (bf16[2,12,2,16,384]{4,3,2,1,0:T(8,128)(2,1)}, bf16[2,12,2,16,384]{4,3,2,1,0:T(8,128)(2,1)S(1)}, u32[]{:S(2)}) copy-start(bf16[2,12,2,16,384]{4,3,2,1,0:T(8,128)(2,1)S(1)} %copy.47) | copy-start | bytes 1769476
  11.8 45.4 %collective-permute-start.5 = (bf16[2,12,32,384]{3,2,1,0:T(8,128)(2,1)S(1)}, bf16[2,12,32,384]{3,2,1,0:T(8,128)(2,1)}, u32[]{:S(2)}, u32[]{:S(2)}) collective-permute-start(bf16[2,12,32,384]{3,2,1,0:T(8,128)(2,1)S(1)} %bitcast.45), channel_id=1, source_target_pairs={{0,32},{1,33},{2,34},{3,35},{4,36},{5,37},{6,38},{7,39},{8,40},{9,... | collective-permute-start | bytes 1769480 | tf_op jit(solution)/shard_map/ppermute | solution.py:467
  12.7 35.7 %copy-start.2 = (bf16[5120,64]{0,1:T(8,128)(2,1)S(1)}, bf16[5120,64]{0,1:T(8,128)(2,1)}, u32[]{:S(2)}) copy-start(bf16[5120,64]{0,1:T(8,128)(2,1)} %param.15) | copy-start | bytes 1966084
  14.2 43.0 %collective-permute-start.3 = (bf16[12,32,384]{2,1,0:T(8,128)(2,1)}, bf16[12,32,384]{2,1,0:T(8,128)(2,1)}, u32[]{:S(2)}, u32[]{:S(2)}) collective-permute-start(bf16[12,32,384]{2,1,0:T(8,128)(2,1)} %collective-permute-done.low), channel_id=1, source_target_pairs={{0,32},{1,33},{2,34},{3,35},{4,36},{5,37},{6,38},{7,39},{8,40},{9,... | collective-permute-start | bytes 884744 | tf_op jit(solution)/shard_map/ppermute | solution.py:468
  18.9 38.3 %collective-permute-start.4 = (bf16[12,32,384]{2,1,0:T(8,128)(2,1)}, bf16[12,32,384]{2,1,0:T(8,128)(2,1)}, u32[]{:S(2)}, u32[]{:S(2)}) collective-permute-start(bf16[12,32,384]{2,1,0:T(8,128)(2,1)} %collective-permute-done.1.high), channel_id=1, source_target_pairs={{0,32},{1,33},{2,34},{3,35},{4,36},{5,37},{6,38},{7,39},{8,40},{9,... | collective-permute-start | bytes 884744 | tf_op jit(solution)/shard_map/ppermute | solution.py:469
  38.1 18.5 %all-to-all-start = ((f32[32,1,768]{2,1,0:T(1,128)}), f32[32,1,768]{2,1,0:T(1,128)S(1)}, u32[]{:S(2)}, u32[]{:S(2)}) async-start(f32[32,1,768]{2,1,0:T(1,128)} %copy.48), calls=%async_computation | async-start | bytes 196608 | tf_op jit(solution)/shard_map/all_to_all | solution.py:480
  71.3 56.5 %collective-permute-start.6 = (bf16[14,96,384]{2,1,0:T(8,128)(2,1)}, bf16[14,96,384]{2,1,0:T(8,128)(2,1)}, u32[]{:S(2)}, u32[]{:S(2)}) collective-permute-start(bf16[14,96,384]{2,1,0:T(8,128)(2,1)} %get-tuple-element.23), channel_id=1, source_target_pairs={{0,1},{1,2},{2,3},{3,0},{4,5},{5,6},{6,7},{7,4},{8,9},{9,10},{10,1... | collective-permute-start | bytes 3096584 | tf_op jit(solution)/shard_map/ppermute | solution.py:434
  72.6 55.3 %collective-permute-start.7 = (bf16[14,96,384]{2,1,0:T(8,128)(2,1)}, bf16[14,96,384]{2,1,0:T(8,128)(2,1)}, u32[]{:S(2)}, u32[]{:S(2)}) collective-permute-start(bf16[14,96,384]{2,1,0:T(8,128)(2,1)} %get-tuple-element.24), channel_id=1, source_target_pairs={{0,2},{1,3},{2,0},{3,1},{4,6},{5,7},{6,4},{7,5},{8,10},{9,11},{10,... | collective-permute-start | bytes 3096584 | tf_op jit(solution)/shard_map/ppermute | solution.py:434
  75.0 52.9 %collective-permute-start.8 = (bf16[14,96,384]{2,1,0:T(8,128)(2,1)}, bf16[14,96,384]{2,1,0:T(8,128)(2,1)}, u32[]{:S(2)}, u32[]{:S(2)}) collective-permute-start(bf16[14,96,384]{2,1,0:T(8,128)(2,1)} %get-tuple-element.25), channel_id=1, source_target_pairs={{0,3},{1,0},{2,1},{3,2},{4,7},{5,4},{6,5},{7,6},{8,11},{9,8},{10,9... | collective-permute-start | bytes 3096584 | tf_op jit(solution)/shard_map/ppermute | solution.py:434
  89.9 23.9 %all-to-all-start.1 = ((bf16[128,2,1472]{2,1,0:T(2,128)(2,1)}), bf16[128,2,1472]{2,1,0:T(2,128)(2,1)S(1)}, u32[]{:S(2)}, u32[]{:S(2)}) async-start(bf16[128,2,1472]{2,1,0:T(2,128)(2,1)} %reshape.186), calls=%async_computation.1 | async-start | bytes 1572864 | tf_op jit(solution)/shard_map/all_to_all | solution.py:484
  121.8 6.0 %copy-start.1 = (bf16[14,96,384]{2,1,0:T(8,128)(2,1)S(1)}, bf16[14,96,384]{2,1,0:T(8,128)(2,1)}, u32[]{:S(2)}) copy-start(bf16[14,96,384]{2,1,0:T(8,128)(2,1)} %get-tuple-element.22) | copy-start | bytes 3096580
  123.0 28.2 %all-to-all-start.2 = ((bf16[128,2,1664]{2,1,0:T(2,128)(2,1)}), bf16[128,2,1664]{2,1,0:T(2,128)(2,1)S(1)}, u32[]{:S(2)}, u32[]{:S(2)}) async-start(bf16[128,2,1664]{2,1,0:T(2,128)(2,1)} %reshape.188), calls=%async_computation.2 | async-start | bytes 1703936 | tf_op jit(solution)/shard_map/all_to_all | solution.py:491
  130.3 14.8 %collective-permute-start.10 = (bf16[14,24,384]{2,1,0:T(8,128)(2,1)S(1)}, bf16[14,24,384]{2,1,0:T(8,128)(2,1)S(1)}, u32[]{:S(2)}, u32[]{:S(2)}) collective-permute-start(bf16[14,24,384]{2,1,0:T(8,128)(2,1)S(1)} %get-tuple-element.28), channel_id=1, source_target_pairs={{0,8},{1,9},{2,10},{3,11},{4,12},{5,13},{6,14},{7,15},{8,0},{9,1},... | collective-permute-start | bytes 774152 | tf_op jit(solution)/shard_map/ppermute | solution.py:437
  133.8 12.1 %collective-permute-start.11 = (bf16[14,24,384]{2,1,0:T(8,128)(2,1)S(1)}, bf16[14,24,384]{2,1,0:T(8,128)(2,1)S(1)}, u32[]{:S(2)}, u32[]{:S(2)}) collective-permute-start(bf16[14,24,384]{2,1,0:T(8,128)(2,1)S(1)} %get-tuple-element.27), channel_id=1, source_target_pairs={{0,12},{1,13},{2,14},{3,15},{4,0},{5,1},{6,2},{7,3},{8,4},{9,5},{1... | collective-permute-start | bytes 774152 | tf_op jit(solution)/shard_map/ppermute | solution.py:437
  134.4 13.3 %collective-permute-start.9 = (bf16[14,24,384]{2,1,0:T(8,128)(2,1)S(1)}, bf16[14,24,384]{2,1,0:T(8,128)(2,1)S(1)}, u32[]{:S(2)}, u32[]{:S(2)}) collective-permute-start(bf16[14,24,384]{2,1,0:T(8,128)(2,1)S(1)} %get-tuple-element.26), channel_id=1, source_target_pairs={{0,4},{1,5},{2,6},{3,7},{4,8},{5,9},{6,10},{7,11},{8,12},{9,13},{1... | collective-permute-start | bytes 774152 | tf_op jit(solution)/shard_map/ppermute | solution.py:437
  147.9 11.3 %collective-permute-start.13 = (bf16[14,12,384]{2,1,0:T(8,128)(2,1)S(1)}, bf16[14,12,384]{2,1,0:T(8,128)(2,1)S(1)}, u32[]{:S(2)}, u32[]{:S(2)}) collective-permute-start(bf16[14,12,384]{2,1,0:T(8,128)(2,1)S(1)} %get-tuple-element.32), channel_id=1, source_target_pairs={{0,16},{1,17},{2,18},{3,19},{4,20},{5,21},{6,22},{7,23},{8,24},{9,... | collective-permute-start | bytes 387080 | tf_op jit(solution)/shard_map/ppermute | solution.py:441
  148.4 10.8 %collective-permute-start.14 = (bf16[14,12,384]{2,1,0:T(8,128)(2,1)S(1)}, bf16[14,12,384]{2,1,0:T(8,128)(2,1)}, u32[]{:S(2)}, u32[]{:S(2)}) collective-permute-start(bf16[14,12,384]{2,1,0:T(8,128)(2,1)S(1)} %get-tuple-element.32), channel_id=1, source_target_pairs={{0,80},{1,81},{2,82},{3,83},{4,84},{5,85},{6,86},{7,87},{8,88},{9,... | collective-permute-start | bytes 387080 | tf_op jit(solution)/shard_map/ppermute | solution.py:442
  150.7 8.5 %collective-permute-start.12 = (bf16[14,12,384]{2,1,0:T(8,128)(2,1)S(1)}, bf16[14,12,384]{2,1,0:T(8,128)(2,1)}, u32[]{:S(2)}, u32[]{:S(2)}) collective-permute-start(bf16[14,12,384]{2,1,0:T(8,128)(2,1)S(1)} %get-tuple-element.31), channel_id=1, source_target_pairs={{0,64},{1,65},{2,66},{3,67},{4,68},{5,69},{6,70},{7,71},{8,72},{9,... | collective-permute-start | bytes 387080 | tf_op jit(solution)/shard_map/ppermute | solution.py:440
  160.3 2.6 %collective-permute-start.15 = (f32[14,12,384]{2,1,0:T(8,128)S(1)}, f32[14,12,384]{2,1,0:T(8,128)S(1)}, u32[]{:S(2)}, u32[]{:S(2)}) collective-permute-start(f32[14,12,384]{2,1,0:T(8,128)S(1)} %add_add_fusion), channel_id=1, source_target_pairs={{0,32},{1,33},{2,34},{3,35},{4,36},{5,37},{6,38},{7,39},{8,40},{9,... | collective-permute-start | bytes 774152 | tf_op jit(solution)/shard_map/ppermute | solution.py:507
